TPU v7x, 128 devices: a whole 4x4x4 slice. The times are simulated.
128 devices in a mesh: krow: 8 (over x, core), tri: 16 (over z, y).
Axes of the slice: x: 4, y: 4, z: 4, core: 2. Of those that a mesh axis runs over, the one named last changes fastest.
Arguments:
- rho_x: bfloat16 [512, 16, 2688], P(('krow', 'tri')), may hold values from -0.83203125 to 0.83203125
- rho_s: bfloat16 [512, 16, 512], P(('krow', 'tri')), may hold values from -1.2578125 to 1.2578125
- coulomb: float32 [2688], replicated, may hold values from 0.1 to 4
- screening: bfloat16 [16, 512, 512], P('tri')
- qmap: int32 [8, 8], replicated, may hold values from 0 to 15, as said below
- qslot: int32 [16], replicated, may hold values from 0 to 15, each once
Outputs:
- kernel: float32 [512, 16, 8192], P(('krow', 'tri'))
Inputs may be any that keep to these rules, and one draw needn't show every extreme that they name: qmap is symmetric; qmap[0, 0] is 0 and qmap[0, 8 - 1] is 15; every screening block is symmetric.
All inputs are finite; a program needn't handle non-finite values.
Results may differ from a plain program's by a relative error of at most 0.0032.
Values may be sent and summed in bfloat16 or wider, within the bound.
A program may use at most 128 MiB of HBM per device.

v0:
```python
import jax
import jax.numpy as jnp
from jax import lax
from jax.sharding import PartitionSpec as P


def body(rho_x, rho_s, coulomb, screening, qmap, qslot):
    kpoints = rho_x.shape[0]
    npair = rho_x.shape[1]
    ntri = lax.axis_size("tri")
    nrows = lax.axis_size("krow")
    group = lax.axis_index("krow")
    scaled = (rho_x.astype(jnp.float32) * jnp.sqrt(coulomb)[None, None, :]).astype(jnp.bfloat16)
    rows_x, rows_s = (
        lax.all_gather(scaled, "tri", axis=0, tiled=True),
        lax.all_gather(rho_s, "tri", axis=0, tiled=True),
    )
    cols_x, cols_s = (
        lax.all_gather(scaled, "krow", axis=0, tiled=True),
        lax.all_gather(rho_s, "krow", axis=0, tiled=True),
    )
    left_x = rows_x.reshape(ntri * kpoints * npair, -1)
    left_s = rows_s.reshape(ntri * kpoints * npair, -1).astype(jnp.float32)
    screens = lax.all_gather(screening, "tri", axis=0, tiled=True)

    def build(wblock, bx, bs):
        exch = jnp.einsum("ag,bg->ab", left_x, bx, preferred_element_type=jnp.float32)
        proj = jnp.einsum("gh,bh->gb", wblock, bs, preferred_element_type=jnp.float32)
        direct = jnp.dot(left_s, proj, precision=lax.Precision.HIGHEST)
        return 2.0 * exch - direct

    def skipped(wblock, bx, bs):
        return jnp.zeros((left_x.shape[0], kpoints * npair), jnp.float32)

    tiles = []
    flags = []
    for other in range(nrows):
        active = group <= other
        wmat = lax.dynamic_index_in_dim(screens, qslot[qmap[group, other]], 0, keepdims=False)
        right_x = lax.dynamic_slice_in_dim(cols_x, other * kpoints, kpoints, 0).reshape(
            kpoints * npair, -1
        )
        right_s = lax.dynamic_slice_in_dim(cols_s, other * kpoints, kpoints, 0).reshape(
            kpoints * npair, -1
        )
        tiles.append(lax.cond(active, build, skipped, wmat, right_x, right_s))
        flags.append(active & (group != other))
    stacked = jnp.stack(tiles)
    count = stacked.shape[0]
    outgoing = stacked.reshape(count, ntri, kpoints, npair, kpoints, npair).transpose(
        1, 2, 3, 0, 4, 5
    )[:, :, :, :, None]
    back = lax.all_to_all(outgoing, "tri", split_axis=0, concat_axis=4, tiled=True)
    owned = back.reshape(kpoints, npair, -1)
    keep = jnp.stack(flags)
    flipped = jnp.where(keep[:, None, None], jnp.swapaxes(stacked, 1, 2), 0.0)
    flipped = flipped.reshape(nrows, kpoints, npair, 1, -1)
    mirrored = lax.all_to_all(flipped, "krow", split_axis=0, concat_axis=3, tiled=True)
    return owned + mirrored.reshape(kpoints, npair, -1)


def solution(mesh):
    placed = (
        P(("krow", "tri"), None, None),
        P(("krow", "tri"), None, None),
        P(),
        P("tri", None, None),
        P(),
        P(),
    )
    return jax.shard_map(
        body, mesh=mesh, in_specs=placed, out_specs=P(("krow", "tri"), None, None), check_vma=False
    )
```

profile of v0, /device:TPU:1, one launch (start us, length us, event | category | flops | bytes accessed | tf_op | source)
XLA Modules:
  0.0 555.7 jit_solution(9641821060480965155)
XLA Ops:
  11.3 14.8 %all_gather.18 = bf16[32,16,512]{2,1,0:T(8,128)(2,1)S(1)} all-gather(bf16[4,16,512]{2,1,0:T(8,128)(2,1)S(1)} %copy-done), channel_id=1, replica_groups=mesh['krow'=8,'tri'=16] {'krow'}, dimensions={0}, use_global_device_ids=true | all-gather | bytes 589824 | tf_op jit(solution)/shard_map/all_gather | solution.py:20
  26.1 28.0 %all-gather.11.cloned.1.call-done = bf16[64,16,512]{2,1,0:T(8,128)(2,1)} async-done(((bf16[4,16,512]{2,1,0:T(8,128)(2,1)}), bf16[64,16,512]{2,1,0:T(8,128)(2,1)}) %all-gather.11.cloned.1.call-update) | async-done | bytes 1048592 | tf_op jit(solution)/shard_map/all_gather | solution.py:16
  55.7 27.7 %all-gather.5.cloned.1.call-done = bf16[32,16,2688]{2,1,0:T(8,128)(2,1)} async-done(((bf16[4,16,2688]{2,1,0:T(8,128)(2,1)}), bf16[32,16,2688]{2,1,0:T(8,128)(2,1)}) %all-gather.5.cloned.1.call-update) | async-done | bytes 2752528 | tf_op jit(solution)/shard_map/all_gather | solution.py:19
  83.3 60.0 %all-gather.7.cloned.1.call-done = bf16[64,16,2688]{2,1,0:T(8,128)(2,1)} async-done(((bf16[4,16,2688]{2,1,0:T(8,128)(2,1)}), bf16[64,16,2688]{2,1,0:T(8,128)(2,1)}) %all-gather.7.cloned.1.call-update) | async-done | bytes 5505040 | tf_op jit(solution)/shard_map/all_gather | solution.py:15
  143.3 72.5 %all-gather.9.cloned.1.call-done = bf16[16,512,512]{2,1,0:T(8,128)(2,1)} async-done(((bf16[1,512,512]{2,1,0:T(8,128)(2,1)}), bf16[16,512,512]{2,1,0:T(8,128)(2,1)}) %all-gather.9.cloned.1.call-update) | async-done | bytes 8388624 | tf_op jit(solution)/shard_map/all_gather | solution.py:24
  215.8 2.6 conditional.8
  220.0 18.3 %conditional.15 = (f32[1,1024,64]{1,2,0:T(8,128)}, f32[1,16,4,16,4,16]{3,2,1,5,4,0:T(4,128)}) conditional(s32[]{:T(128)} %convert_element_type.47, () %tuple.213, (bf16[32,16,2688]{2,1,0:T(8,128)(2,1)}, bf16[1024,2688]{1,0:T(8,128)(2,1)}, s32[8,8]{1,0:T(8,128)S(1)}, s32[]{:T(128)}, s32[16]{0:T(128)S(1)}, ...), branch_computations={%region_14.15_spmd, %region_15.16_spmd} | conditional | flops 788660224 | bytes 10928240 | solution.py:46
  226.4 2.1 convolution_bitcast_fusion.7
  229.6 5.0 fusion.35
  234.6 3.7 stack.148
  238.4 18.7 %conditional.14 = (f32[1,1024,64]{1,2,0:T(8,128)}, f32[1,16,4,16,4,16]{3,2,1,5,4,0:T(4,128)}) conditional(s32[]{:T(128)} %convert_element_type.46, () %tuple.212, (bf16[32,16,2688]{2,1,0:T(8,128)(2,1)}, bf16[1024,2688]{1,0:T(8,128)(2,1)}, s32[8,8]{1,0:T(8,128)S(1)}, s32[]{:T(128)}, s32[16]{0:T(128)S(1)}, ...), branch_computations={%region_12.13_spmd, %region_13.14_spmd} | conditional | flops 788660224 | bytes 10928240 | solution.py:46
  245.2 2.1 convolution_bitcast_fusion.6
  248.3 5.0 fusion.30
  253.3 3.7 stack.144
  257.1 18.3 %conditional.13 = (f32[1,1024,64]{1,2,0:T(8,128)}, f32[1,16,4,16,4,16]{3,2,1,5,4,0:T(4,128)}) conditional(s32[]{:T(128)} %convert_element_type.45, () %tuple.211, (bf16[32,16,2688]{2,1,0:T(8,128)(2,1)}, bf16[1024,2688]{1,0:T(8,128)(2,1)}, s32[8,8]{1,0:T(8,128)S(1)}, s32[]{:T(128)}, s32[16]{0:T(128)S(1)}, ...), branch_computations={%region_10.11_spmd, %region_11.12_spmd} | conditional | flops 788660224 | bytes 10928240 | solution.py:46
  263.5 2.1 convolution_bitcast_fusion.5
  266.6 5.0 fusion.25
  271.7 3.8 stack.140
  275.4 18.4 %conditional.12 = (f32[1,1024,64]{1,2,0:T(8,128)}, f32[1,16,4,16,4,16]{3,2,1,5,4,0:T(4,128)}) conditional(s32[]{:T(128)} %convert_element_type.44, () %tuple.210, (bf16[32,16,2688]{2,1,0:T(8,128)(2,1)}, bf16[1024,2688]{1,0:T(8,128)(2,1)}, s32[8,8]{1,0:T(8,128)S(1)}, s32[]{:T(128)}, s32[16]{0:T(128)S(1)}, /*index=5*/bf16[16,512,512]{2,1,0:T(8,128)(2,1)}, ...), branch_computations={%region_8.9_spmd, %region_9.10_spmd} | conditional | flops 788660224 | bytes 10928240 | solution.py:46
  281.8 2.1 convolution_bitcast_fusion.4
  284.9 5.0 fusion.20
  290.0 3.8 stack.136
  293.8 18.6 %conditional.11 = (f32[1,1024,64]{1,2,0:T(8,128)}, f32[1,16,4,16,4,16]{3,2,1,5,4,0:T(4,128)}) conditional(s32[]{:T(128)} %convert_element_type.43, () %tuple.209, (bf16[32,16,2688]{2,1,0:T(8,128)(2,1)}, bf16[1024,2688]{1,0:T(8,128)(2,1)}, s32[8,8]{1,0:T(8,128)S(1)}, s32[]{:T(128)}, s32[16]{0:T(128)S(1)}, /*index=5*/bf16[16,512,512]{2,1,0:T(8,128)(2,1)}, ...), branch_computations={%region_6.7_spmd, %region_7.8_spmd} | conditional | flops 788660224 | bytes 10928240 | solution.py:46
  300.3 2.1 convolution_bitcast_fusion.3
  303.5 5.0 fusion.15
  308.5 3.8 stack.132
  312.3 18.4 %conditional.10 = (f32[1,1024,64]{1,2,0:T(8,128)}, f32[1,16,4,16,4,16]{3,2,1,5,4,0:T(4,128)}) conditional(s32[]{:T(128)} %convert_element_type.42, () %tuple.208, (bf16[32,16,2688]{2,1,0:T(8,128)(2,1)}, bf16[1024,2688]{1,0:T(8,128)(2,1)}, s32[8,8]{1,0:T(8,128)S(1)}, s32[]{:T(128)}, s32[16]{0:T(128)S(1)}, /*index=5*/bf16[16,512,512]{2,1,0:T(8,128)(2,1)}, ...), branch_computations={%region_4.5_spmd, %region_5.6_spmd} | conditional | flops 788660224 | bytes 10928240 | solution.py:46
  318.7 2.1 convolution_bitcast_fusion.2
  321.9 5.0 fusion.10
  326.9 3.8 stack.128
  330.7 18.5 %conditional.9 = (f32[1,1024,64]{1,2,0:T(8,128)}, f32[1,16,4,16,4,16]{3,2,1,5,4,0:T(4,128)}) conditional(s32[]{:T(128)} %convert_element_type.41, () %tuple.207, (bf16[32,16,2688]{2,1,0:T(8,128)(2,1)}, bf16[1024,2688]{1,0:T(8,128)(2,1)}, s32[8,8]{1,0:T(8,128)S(1)}, s32[]{:T(128)}, s32[16]{0:T(128)S(1)}, /*index=5*/bf16[16,512,512]{2,1,0:T(8,128)(2,1)}, ...), branch_computations={%region_2.3_spmd, %region_3.4_spmd} | conditional | flops 788660224 | bytes 10928240 | solution.py:46
  337.3 2.1 convolution_bitcast_fusion.1
  340.4 5.0 fusion.5
  345.5 3.8 stack.124
  361.0 3.3 broadcast_select_fusion
  364.2 19.9 %all-to-all-start.1 = ((f32[8,4,16,1,1024]{4,2,1,3,0:T(8,128)}), f32[8,4,16,1,1024]{4,2,1,3,0:T(8,128)S(1)}, u32[]{:S(2)}, u32[]{:S(2)}) async-start(f32[8,4,16,1,1024]{4,2,1,3,0:T(8,128)} %bitcast.186), calls=%async_computation.1 | async-start | bytes 4194304 | tf_op jit(solution)/shard_map/all_to_all | solution.py:58
  399.7 8.5 %copy.31 = f32[8,16,4,16,4,16]{3,2,5,4,0,1:T(4,128)} copy(f32[8,16,4,16,4,16]{3,2,1,5,4,0:T(4,128)S(1)} %constant_dynamic-update-slice_fusion) | data formatting | bytes 4194304 | tf_op jit(solution)/shard_map/stack | solution.py:48
  408.2 18.8 %reshape.225 = f32[16,1,32768]{2,1,0:T(1,128)} reshape(f32[16,1,8,4,16,4,16]{6,5,4,3,2,1,0:T(4,128)} %bitcast.184) | data formatting | bytes 4194304
  427.0 5.4 all-to-all-start
  432.4 2.5 copy.26
  434.9 2.7 reshape.223
  437.7 27.9 %all-to-all-done = f32[16,1,32768]{2,1,0:T(1,128)} async-done(((f32[16,1,32768]{2,1,0:T(1,128)}), f32[16,1,32768]{2,1,0:T(1,128)}, u32[]{:S(2)}, u32[]{:S(2)}) %all-to-all-start) | async-done | bytes 2097184 | tf_op jit(solution)/shard_map/all_to_all | solution.py:53
  466.1 7.3 %reduce = f32[16,32768]{1,0:T(8,128)S(1)} reduce(f32[16,1,32768]{2,1,0:T(1,128)} %all-to-all-done, f32[]{:T(128)} %broadcast.133), dimensions={1}, to_apply=%all_to_all.22.reduce_sub_computation | reduce | bytes 4194308 | tf_op jit(solution)/shard_map/all_to_all | solution.py:53
  473.4 17.9 %reshape.226 = f32[16,1,8,4,16,4,16]{6,5,4,3,2,1,0:T(4,128)} reshape(f32[16,32768]{1,0:T(8,128)S(1)} %reduce) | data formatting | bytes 4194304
  491.4 14.1 %bitcast_bitcast_fusion = f32[1,4,16,8,16,1,4,16]{2,1,7,6,3,4,5,0:T(4,128)} fusion(f32[16,1,8,4,16,4,16]{6,5,4,3,2,1,0:T(4,128)} %reshape.226), kind=kLoop, calls=%fused_computation.84 | loop fusion | bytes 4194304 | tf_op jit(solution)/shard_map/all_to_all | solution.py:53
  505.5 21.6 %copy.25 = f32[1,4,16,8,16,1,4,16]{7,6,4,3,2,1,5,0:T(4,128)} copy(f32[1,4,16,8,16,1,4,16]{2,1,7,6,3,4,5,0:T(4,128)} %bitcast_bitcast_fusion) | data formatting | bytes 4194304 | tf_op jit(solution)/shard_map/all_to_all | solution.py:53
  527.0 18.6 %reshape.221 = f32[4,16,8192]{2,1,0:T(8,128)S(1)} reshape(f32[1,4,16,8,16,1,4,16]{7,6,4,3,2,1,5,0:T(4,128)} %copy.25) | data formatting | bytes 4194304 | tf_op jit(solution)/shard_map/reshape | solution.py:54
  545.6 3.1 add.127
  (73 shorter events, 63.6 us)
Async XLA Ops:
  6.5 4.8 copy-start
  6.5 47.6 %all-gather.11.cloned.1.call-start = ((), (), s32[]{:S(2)}) async-start(), calls=%async_computation.5 | async-start | bytes 1114112 | tf_op jit(solution)/shard_map/all_gather | solution.py:16
  7.3 76.1 %all-gather.5.cloned.1.call-start = ((), (), s32[]{:S(2)}) async-start(), calls=%async_computation.2 | async-start | bytes 3096576 | tf_op jit(solution)/shard_map/all_gather | solution.py:19
  9.8 133.5 %all-gather.7.cloned.1.call-start = ((), (), s32[]{:S(2)}) async-start(), calls=%async_computation.3 | async-start | bytes 5849088 | tf_op jit(solution)/shard_map/all_gather | solution.py:15
  10.6 205.2 %copy-start.1 = (s32[8,8]{1,0:T(8,128)S(1)}, s32[8,8]{1,0:T(8,128)}, u32[]{:S(2)}) copy-start(s32[8,8]{1,0:T(8,128)} %param.26) | copy-start | bytes 772
  10.6 205.2 %copy-start.2 = (s32[16]{0:T(128)S(1)}, s32[16]{0:T(128)}, u32[]{:S(2)}) copy-start(s32[16]{0:T(128)} %param.27) | copy-start | bytes 196
  10.6 205.2 %all-gather.9.cloned.1.call-start = ((), (), s32[]{:S(2)}) async-start(), calls=%async_computation.4 | async-start | bytes 8912896 | tf_op jit(solution)/shard_map/all_gather | solution.py:24
  364.2 62.8 %all-to-all-start.1 = ((f32[8,4,16,1,1024]{4,2,1,3,0:T(8,128)}), f32[8,4,16,1,1024]{4,2,1,3,0:T(8,128)S(1)}, u32[]{:S(2)}, u32[]{:S(2)}) async-start(f32[8,4,16,1,1024]{4,2,1,3,0:T(8,128)} %bitcast.186), calls=%async_computation.1 | async-start | bytes 4194304 | tf_op jit(solution)/shard_map/all_to_all | solution.py:58
  427.0 38.6 %all-to-all-start = ((f32[16,1,32768]{2,1,0:T(1,128)}), f32[16,1,32768]{2,1,0:T(1,128)}, u32[]{:S(2)}, u32[]{:S(2)}) async-start(f32[16,1,32768]{2,1,0:T(1,128)} %reshape.225), calls=%async_computation | async-start | bytes 4194304 | tf_op jit(solution)/shard_map/all_to_all | solution.py:53
Sparse Core Ops, SparseCore 0:
  9.5 44.6 all-gather.10
  55.8 27.4 all-gather.4
  85.5 57.7 all-gather.6
  145.3 70.4 all-gather.8
where the time goes:
time: 566 us; the launch traced here: 556 us
  waiting for transfers between devices  218 us (39%)
  local copies, waits for them, and re-layouts  180 us (32%)
  matrix products  59.5 us (11%)
  loops' own time  27.1 us (5%)
  starting transfers between devices  25.4 us (4%)
  other arithmetic  17 us (3%)
  blocking collectives  14.8 us (3%)
  between operations  13.7 us (2%)
    all_gather x1, waiting for transfers between devices, body(): screens = lax.all_gather(screening, 'tri', axis=0, tiled=True)  72.5 us
    unnamed x22, local copies, waits for them, and re-layouts  62 us
    all_gather x1, waiting for transfers between devices, body(): lax.all_gather(scaled, 'tri', axis=0, tiled=True)  60 us
    another operation x12, local copies, waits for them, and re-layouts, body(): stacked = jnp.stack(tiles)  41.2 us
    all_to_all x3, local copies, waits for them, and re-layouts, body(): lax.all_to_all(outgoing, 'tri', split_axis=0, concat_axis=4, tiled=True)  36.2 us
    dot_general x7, matrix products, build(): jnp.einsum('ag,bg->ab', left_x, bx, preferred_element_type=jnp.float32)  35.3 us
    all_gather x1, waiting for transfers between devices, body(): lax.all_gather(rho_s, 'tri', axis=0, tiled=True)  28 us
    all_to_all x1, waiting for transfers between devices, body(): lax.all_to_all(outgoing, 'tri', split_axis=0, concat_axis=4, tiled=True)  27.9 us
  transfers between devices with their start and end apart: 6, of which 5 were waited for; matrix products, arithmetic and copies ran while one was open for 9% of the time, Pallas kernels for 0%

commit v1 on v0

v1 whole, which is shorter than its diff:
```python
import functools

import jax
import jax.numpy as jnp
from jax import lax
from jax.experimental import pallas as pl
from jax.experimental.pallas import tpu as pltpu
from jax.sharding import PartitionSpec as P

MESH = pl.DeviceIdType.MESH
SIDE = 4
CORES = 2
GROUPS = SIDE * CORES
PLANE = SIDE * SIDE

ROWS = ((0, 0), (0, 2), (0, 1), (1, 0), (1, 1), (1, 3), (2, 0), (2, 2), (3, 2), (2, 3))
PAIRS = (2, 4, 8)
EARLY = 6
ROW_FROM = {
    (0, 1): (0, 1), (0, 2): (0, 1), (1, 0): (1, 0), (2, 0): (1, 0), (1, 3): (0, 3),
    (3, 2): (3, 0), (2, 2): (3, 0), (2, 3): (0, 3),
}
W_FROM = {
    (0, 3): (0, 3), (0, 2): (0, 3), (0, 1): (0, 1),
    (3, 0): (3, 0), (3, 1): (3, 0), (3, 2): (3, 0), (3, 3): (3, 0),
    (1, 0): (1, 0), (1, 1): (0, 1), (1, 3): (0, 3), (1, 2): (0, 3),
    (2, 0): (3, 0), (2, 3): (0, 3), (2, 2): (3, 0), (2, 1): (1, 0),
}


def row_from(b, k):
    if b == (1, 1):
        return (1, 0) if k < 2 else (0, 1)
    return ROW_FROM[b]


def less(b, e):
    return ((b[0] - e[0]) % SIDE, (b[1] - e[1]) % SIDE)


def depth(b, source):
    return 0 if b == (0, 0) else 1 + depth(less(b, source(b)), source)


def kernel(parts, rx, rs, cou, w, qmap, qslot, out,
           srow, xrow, scol, xcol, wst, pt, ysend, y, rout, tout, tin, inb, acc, ssem, rsem):
    nb, width = rs.shape
    chunk = xrow.shape[2]
    kr = lax.axis_index("krow")
    tr = lax.axis_index("tri")
    px, pc = kr // CORES, kr % CORES
    pz, py = tr // SIDE, tr % SIDE

    def plane_at(b):
        return ((pz + b[1]) % SIDE) * SIDE + (py + b[0]) % SIDE

    def line_at(dx, dc):
        return ((px + dx) % SIDE) * CORES + (pc + dc) % CORES

    def block(index):
        return pl.ds(pl.multiple_of(index * nb, nb), nb)

    def row(k, slot):
        rows = pl.ds(slot * nb, nb)
        return srow.at[rows] if k == 0 else xrow.at[k - 1, rows]

    def col(k, o):
        return scol.at[block(o)] if k == 0 else xcol.at[k - 1, block(o)]

    line = [(dx, dc) for dx in range(SIDE) for dc in range(CORES) if (dx, dc) != (0, 0)]
    others = [(dy, dz) for dy in range(SIDE) for dz in range(SIDE) if (dy, dz) != (0, 0)]

    barrier = pltpu.get_barrier_semaphore()
    for b in others:
        pl.semaphore_signal(barrier, inc=1, device_id={"tri": plane_at(b)}, device_id_type=MESH)
    for dx, dc in line:
        pl.semaphore_signal(barrier, inc=1, device_id={"krow": line_at(dx, dc)}, device_id_type=MESH)

    wst[tr] = w[block(kr), :]
    srow[0:nb, :] = rs[...]
    scol[block(kr), :] = rs[...]

    def scale(k):
        lanes = pl.ds((k - 1) * chunk, chunk)
        own = (rx[:, lanes].astype(jnp.float32) * jnp.sqrt(cou[:, lanes])).astype(jnp.bfloat16)
        xrow[k - 1, 0:nb, :] = own
        xcol[k - 1, block(kr), :] = own

    scale(1)
    pl.semaphore_wait(barrier, len(others) + len(line))

    copies = {}

    def send(name, src, dst, device):
        i = len(copies)
        copies[name] = pltpu.make_async_remote_copy(
            src_ref=src, dst_ref=dst, send_sem=ssem.at[i], recv_sem=rsem.at[i],
            device_id=device, device_id_type=MESH,
        )
        copies[name].start()

    def send_w(parent):
        for b, e in W_FROM.items():
            if less(b, e) == parent:
                held = wst.at[plane_at(parent)]
                send(("w", b), held, held, {"tri": plane_at((-e[0], -e[1]))})

    def send_row(parent, k):
        for slot, b in enumerate(ROWS):
            if slot and less(b, row_from(b, k)) == parent:
                e = row_from(b, k)
                send(("row", b, k), row(k, ROWS.index(parent)), row(k, slot), {"tri": plane_at((-e[0], -e[1]))})

    def send_col(k):
        for dx in (1, 3, 2):
            send(("col", dx, k), col(k, kr), col(k, kr), {"krow": line_at(-dx, 0)})
        send_sib(0, k)

    def send_sib(dx, k):
        held = col(k, line_at(dx, 0))
        send(("sib", dx, k), held, held, {"krow": line_at(0, 1)})

    def project():
        pt[...] = (
            lax.dot_general(
                wst[...].reshape(PLANE * nb, width), scol[...], (((1,), (1,)), ((), ())),
                preferred_element_type=jnp.float32,
            ) * -0.5
        ).astype(jnp.bfloat16).reshape(pt.shape)
        low = lax.broadcasted_iota(jnp.int32, (nb, 2 * nb), 1) < nb
        for dx, dc in line + [(0, 0)]:
            o = line_at(dx, dc)
            for q in range(GROUPS // 2):
                lanes = pl.ds(q * 2 * nb, 2 * nb)
                first = pt[qslot[qmap[o, 2 * q]], :, lanes]
                second = pt[qslot[qmap[o, 2 * q + 1]], :, lanes]
                ysend[o, :, lanes] = jnp.where(low, first, second)
            if (dx, dc) == (0, 0):
                y[block(kr), :] = ysend[kr]
            else:
                send(("y", dx, dc), ysend.at[o], y.at[block(kr)], {"krow": o})

    def rows_of(group):
        return slice(0, EARLY * nb) if group == 0 else slice(EARLY * nb, len(ROWS) * nb)

    def exchange(group, k):
        rows = rows_of(group)
        part = lax.dot_general(
            xrow[k - 1, rows, :], xcol[k - 1], (((1,), (1,)), ((), ())), preferred_element_type=jnp.float32
        )
        acc[rows, :] = part if k == 1 else acc[rows, :] + part

    def finish(group):
        rows = rows_of(group)
        total = acc[rows, :] + jnp.dot(srow[rows, :], y[...], preferred_element_type=jnp.float32)
        acc[rows, :] = total * 2.0
        rout[rows, :] = acc[rows, :].astype(jnp.bfloat16)
        for slot in range(0, EARLY) if group == 0 else range(EARLY, len(ROWS)):
            if slot == 0:
                inb[tr] = rout[0:nb, :]
            else:
                b = ROWS[slot]
                send(("out", b), rout.at[pl.ds(slot * nb, nb)], inb.at[tr], {"tri": plane_at(b)})
        pairs = [i for i, p in enumerate(PAIRS) if (p < EARLY) == (group == 0)]
        for i in pairs:
            p = PAIRS[i]
            tout[i] = acc[p * nb : (p + 2) * nb, :].T.astype(jnp.bfloat16)
            tin[i, block(kr), :] = tout[i, block(kr), :]
            for dx, dc in line:
                o = line_at(dx, dc)
                send(("flip", i, dx, dc), tout.at[i, block(o)], tin.at[i, block(kr)], {"krow": o})

    events = []
    for b in W_FROM:
        events.append((2.0 * depth(b, W_FROM.get), ("w", b)))
    for k in range(parts + 1):
        for b in ROWS[1:]:
            events.append((3.0 + 2.5 * k + 4.0 * depth(b, lambda v: row_from(v, k)), ("row", b, k)))
        for dx in (1, 3, 2):
            events.append((3.5 + 4.5 * k + (0.5 if dx == 2 else 0), ("col", dx, k)))
        for dx in range(SIDE):
            events.append((5.5 + 4.5 * k, ("sib", dx, k)))
    for dx, dc in line:
        events.append((15.0, ("y", dx, dc)))
    events.sort(key=lambda v: v[0])

    def names(kind, k=None):
        return [name for _, name in events if name[0] == kind and (k is None or name[-1] == k)]

    def group_rows(group, k):
        return [n for n in names("row", k) if (ROWS.index(n[1]) < EARLY) == (group == 0)]

    tasks = [(names("w") + names("col", 0) + names("sib", 0), project)]
    for k in range(1, parts + 1):
        for group in range(2):
            tasks.append(
                (group_rows(group, k) + names("col", k) + names("sib", k), functools.partial(exchange, group, k))
            )
    for group in range(2):
        deps = names("y")
        for k in range(parts + 1):
            deps = deps + group_rows(group, k) + names("col", k) + names("sib", k)
        tasks.append((deps, functools.partial(finish, group)))

    send_w((0, 0))
    send_col(0)
    send_row((0, 0), 0)
    for k in range(1, parts + 1):
        if k > 1:
            scale(k)
        send_col(k)
        send_row((0, 0), k)

    seen = set()
    for _, name in events:
        copies[name].wait_recv()
        seen.add(name)
        if name[0] == "w":
            send_w(name[1])
        elif name[0] == "row":
            send_row(name[1], name[2])
        elif name[0] == "col":
            send_sib(name[1], name[2])
        for task in [t for t in tasks if seen.issuperset(t[0])]:
            task[1]()
            tasks.remove(task)

    low = lax.broadcasted_iota(jnp.int32, (nb, 2 * nb), 1) < nb

    def mix(first, second):
        return (
            jnp.where(low, first, pltpu.roll(second, nb, 1)),
            jnp.where(low, pltpu.roll(first, nb, 1), second),
        )

    for i, p in enumerate(PAIRS):
        for dx, dc in line:
            copies["flip", i, dx, dc].wait_recv()
        for q in range(GROUPS // 2):
            first = tin[i, 2 * q * nb : (2 * q + 1) * nb, :].astype(jnp.float32)
            second = tin[i, (2 * q + 1) * nb : (2 * q + 2) * nb, :].astype(jnp.float32)
            for slot, got in zip((p, p + 1), mix(first, second)):
                inb[plane_at(ROWS[slot]), :, q * 2 * nb : (q + 1) * 2 * nb] = got.astype(jnp.bfloat16)
    for b in ROWS[1:]:
        copies["out", b].wait_recv()
    span = PLANE * nb
    for m in range(PLANE // 2):
        for q in range(GROUPS // 2):
            lanes = slice(q * 2 * nb, (q + 1) * 2 * nb)
            first = inb[2 * m, :, lanes].astype(jnp.float32)
            second = inb[2 * m + 1, :, lanes].astype(jnp.float32)
            for o, got in zip((2 * q, 2 * q + 1), mix(first, second)):
                at = o * span + m * 2 * nb
                out[:, at : at + 2 * nb] = got
    for copy in copies.values():
        copy.wait_send()


def body(rho_x, rho_s, coulomb, screening, qmap, qslot):
    kpoints, npair, waves = rho_x.shape
    width = rho_s.shape[-1]
    nb = kpoints * npair
    parts = 3
    chunk = waves // parts
    cols = GROUPS * nb
    bf16, f32 = jnp.bfloat16, jnp.float32
    vmem = pl.BlockSpec(memory_space=pltpu.VMEM)
    smem = pl.BlockSpec(memory_space=pltpu.SMEM)
    ncopies = 15 + 9 * (parts + 1) + 7 * (parts + 1) + 7 + 9 + 21
    out = pl.pallas_call(
        functools.partial(kernel, parts),
        out_shape=jax.ShapeDtypeStruct((nb, GROUPS * PLANE * nb), f32),
        in_specs=[vmem, vmem, vmem, vmem, smem, smem],
        out_specs=vmem,
        scratch_shapes=[
            pltpu.VMEM((len(ROWS) * nb, width), bf16),
            pltpu.VMEM((parts, len(ROWS) * nb, chunk), bf16),
            pltpu.VMEM((cols, width), bf16),
            pltpu.VMEM((parts, cols, chunk), bf16),
            pltpu.VMEM((PLANE, nb, width), bf16),
            pltpu.VMEM((PLANE, nb, cols), bf16),
            pltpu.VMEM((GROUPS, nb, cols), bf16),
            pltpu.VMEM((width, cols), bf16),
            pltpu.VMEM((len(ROWS) * nb, cols), bf16),
            pltpu.VMEM((len(PAIRS), cols, 2 * nb), bf16),
            pltpu.VMEM((len(PAIRS), cols, 2 * nb), bf16),
            pltpu.VMEM((PLANE, nb, cols), bf16),
            pltpu.VMEM((len(ROWS) * nb, cols), f32),
            pltpu.SemaphoreType.DMA((ncopies,)),
            pltpu.SemaphoreType.DMA((ncopies,)),
        ],
        compiler_params=pltpu.CompilerParams(
            collective_id=0, has_side_effects=True, vmem_limit_bytes=48 * 2**20
        ),
        name="kernel_rows",
    )(
        rho_x.reshape(nb, waves),
        rho_s.reshape(nb, width),
        coulomb.reshape(1, waves),
        screening.reshape(width, width),
        qmap,
        qslot,
    )
    return out.reshape(kpoints, npair, -1)


def solution(mesh):
    placed = (
        P(("krow", "tri"), None, None),
        P(("krow", "tri"), None, None),
        P(),
        P("tri", None, None),
        P(),
        P(),
    )
    return jax.shard_map(
        body, mesh=mesh, in_specs=placed, out_specs=P(("krow", "tri"), None, None), check_vma=False
    )
```

time: 566 us -> 70.8 us (0.13); the launches traced: 556 us -> 70.4 us
  waiting for transfers between devices: 218 us -> 0 us
  local copies, waits for them, and re-layouts: 180 us -> 6.23 us
  Pallas kernels: 0 us -> 64.1 us
  matrix products: 59.5 us -> 0 us
  loops' own time: 27.1 us -> 0 us
  starting transfers between devices: 25.4 us -> 0 us
  other arithmetic: 17 us -> 0 us
  blocking collectives: 14.8 us -> 0 us
  between operations: 13.7 us -> 0.02 us
    all_gather x4 -> x0, waiting for transfers between devices: 188 us -> none  [the longest x1 72.5 us: body(): screens = lax.all_gather(screening, 'tri', axis=0, tiled=True)]
    pallas_call x0 -> x1, Pallas kernels: none -> 64.1 us  [body(): pl.pallas_call(functools.partial(kernel, parts), out_shape=jax.ShapeDtype...]
    dot_general x21 -> x0, matrix products: 59.5 us -> none  [the longest x7 35.3 us: build(): jnp.einsum('ag,bg->ab', left_x, bx, preferred_element_type=jnp.float32)]
    unnamed x22 -> x11, local copies, waits for them, and re-layouts: 62 us -> 5.52 us
    another operation x13 -> x0, local copies, waits for them, and re-layouts: 41.3 us -> none  [the longest x12 41.2 us: body(): stacked = jnp.stack(tiles)]
    all_to_all x4 -> x0, local copies, waits for them, and re-layouts: 38.7 us -> none  [the longest x3 36.2 us: body(): lax.all_to_all(outgoing, 'tri', split_axis=0, concat_axis=4, tiled=True)]
    all_to_all x2 -> x0, waiting for transfers between devices: 27.9 us -> none  [the longest x1 27.9 us: body(): lax.all_to_all(outgoing, 'tri', split_axis=0, concat_axis=4, tiled=True)]
    another operation x8 -> x0, loops' own time: 27.1 us -> none  [body(): tiles.append(lax.cond(active, build, skipped, wmat, right_x, right_s))]
  transfers between devices with their start and end apart: 6 -> 0, of which waited for: 5 -> 0; matrix products, arithmetic and copies ran while one was open for 9% -> 0% of each run, Pallas kernels for 0% -> 0%
where the time goes in v1:
time: 70.8 us; the launch traced here: 70.4 us
  Pallas kernels  64.1 us (91%)
  local copies, waits for them, and re-layouts  6.23 us (9%)
    pallas_call x1, Pallas kernels, body(): pl.pallas_call(functools.partial(kernel, parts), out_shape=jax.ShapeDtype...  64.1 us
    unnamed x11, local copies, waits for them, and re-layouts  5.52 us

profile of v1, /device:TPU:1, one launch (start us, length us, event | category | flops | bytes accessed | tf_op | source)
XLA Modules:
  0.0 70.4 jit_solution(8164410735522680464)
XLA Ops:
  0.0 0.7 %reshape.17.cou = f32[1,2688]{1,0:T(1,128)S(1)} reshape(f32[2688]{0:T(1024)} %param.8) | data formatting | bytes 21504 | tf_op jit(solution)/shard_map/reshape | solution.py:299
  0.7 0.0 copy-start
  0.7 1.0 %copy-done = bf16[1,512,512]{2,1,0:T(8,128)(2,1)S(1)} copy-done((bf16[1,512,512]{2,1,0:T(8,128)(2,1)S(1)}, bf16[1,512,512]{2,1,0:T(8,128)(2,1)}, u32[]{:S(2)}) %copy-start) | copy-done | bytes 524312
  1.8 0.0 copy-start.1
  1.8 1.0 %copy-done.1 = bf16[4,16,2688]{2,1,0:T(8,128)(2,1)S(1)} copy-done((bf16[4,16,2688]{2,1,0:T(8,128)(2,1)S(1)}, bf16[4,16,2688]{2,1,0:T(8,128)(2,1)}, u32[]{:S(2)}) %copy-start.1) | copy-done | bytes 344088
  2.7 0.0 copy-start.2
  2.7 0.8 %copy-done.2 = bf16[4,16,512]{2,1,0:T(8,128)(2,1)S(1)} copy-done((bf16[4,16,512]{2,1,0:T(8,128)(2,1)S(1)}, bf16[4,16,512]{2,1,0:T(8,128)(2,1)}, u32[]{:S(2)}) %copy-start.2) | copy-done | bytes 65560
  3.6 0.0 copy-start.3
  3.6 0.7 copy-done.3
  4.3 0.0 copy-start.4
  4.3 0.7 copy-done.4
  4.9 64.1 %kernel_rows.1 = f32[64,8192]{1,0:T(8,128)S(1)} custom-call(bf16[64,2688]{1,0:T(8,128)(2,1)S(1)} %bitcast.6, bf16[64,512]{1,0:T(8,128)(2,1)S(1)} %bitcast.7, f32[1,2688]{1,0:T(1,128)S(1)} %reshape.17.cou, bf16[512,512]{1,0:T(8,128)(2,1)S(1)} %bitcast.5, s32[8,8]{1,0:T(8,128)S(1)} %copy-done.3, s32[16]{0:T(128)S(1)} %copy-done.4), custom_call_target="tpu_custom_call" | custom-call | tf_op jit(solution)/shard_map/kernel_rows/pallas_call | solution.py:270
  69.0 1.3 %copy.8 = f32[4,16,8192]{2,1,0:T(8,128)} copy(f32[4,16,8192]{2,1,0:T(8,128)S(1)} %bitcast.4) | data formatting | bytes 4194304
Async XLA Ops:
  0.7 1.0 %copy-start = (bf16[1,512,512]{2,1,0:T(8,128)(2,1)S(1)}, bf16[1,512,512]{2,1,0:T(8,128)(2,1)}, u32[]{:S(2)}) copy-start(bf16[1,512,512]{2,1,0:T(8,128)(2,1)} %param.9) | copy-start | bytes 1572868
  1.8 1.0 %copy-start.1 = (bf16[4,16,2688]{2,1,0:T(8,128)(2,1)S(1)}, bf16[4,16,2688]{2,1,0:T(8,128)(2,1)}, u32[]{:S(2)}) copy-start(bf16[4,16,2688]{2,1,0:T(8,128)(2,1)} %param.6) | copy-start | bytes 1032196
  2.7 0.8 %copy-start.2 = (bf16[4,16,512]{2,1,0:T(8,128)(2,1)S(1)}, bf16[4,16,512]{2,1,0:T(8,128)(2,1)}, u32[]{:S(2)}) copy-start(bf16[4,16,512]{2,1,0:T(8,128)(2,1)} %param.7) | copy-start | bytes 196612
  3.6 0.7 copy-start.3
  4.3 0.7 copy-start.4

commit v2 on v1

v2 whole, which is shorter than its diff:
```python
import functools

import jax
import jax.numpy as jnp
from jax import lax
from jax.experimental import pallas as pl
from jax.experimental.pallas import tpu as pltpu
from jax.sharding import PartitionSpec as P

MESH = pl.DeviceIdType.MESH
SIDE = 4
CORES = 2
GROUPS = SIDE * CORES
PLANE = SIDE * SIDE

ROWS = ((0, 0), (2, 0), (3, 0), (0, 3), (1, 3), (0, 2), (2, 1), (1, 2), (2, 2), (1, 1))
PLAN = {
    (0, 1): (
        (0, 1, -1), (0, 2, -1), (1, 1, -1), (2, 1, -1), (3, 2, -1), (1, 2, -1), (2, 2, -1), (3, 3, -1),
        (2, 1, 0), (2, 1, 1), (2, 2, 0), (2, 1, 3), (2, 1, 2), (2, 2, 3),
    ),
    (1, 0): (
        (1, 0, -1), (2, 0, -1), (1, 3, -1), (1, 3, 2), (1, 3, 1), (2, 3, -1), (1, 2, 2), (1, 2, 1),
        (1, 3, 3), (1, 3, 0), (2, 2, 1), (2, 2, 2),
    ),
    (0, 3): (
        (0, 3, -1), (0, 3, 2), (0, 3, 1), (0, 2, 2), (0, 2, 1), (3, 0, -1), (0, 3, 3), (0, 3, 0),
        (1, 1, 2), (0, 2, 3), (0, 2, 0), (1, 2, 3),
    ),
    (3, 0): (
        (3, 0, 1), (3, 0, 0), (3, 1, -1), (2, 0, 1), (2, 0, 0), (3, 0, 3), (3, 0, 2), (2, 0, 3),
        (2, 0, 2), (1, 1, 0), (1, 1, 1), (1, 2, 0), (1, 1, 3),
    ),
}
OUT = tuple(i for i, b in enumerate(ROWS) if i == 1 or b[0] % 2 or b[1] % 2)
FLIP = (2, 4, 6, 8)
PARTS = 3
RATE = 9e4
LATENCY = 1.9
WINDOW = 4


def less(b, e):
    return ((b[0] - e[0]) % SIDE, (b[1] - e[1]) % SIDE)


def transfers(parts, cost):
    links = {}
    for e, entries in PLAN.items():
        links[e] = []
        for dy, dz, k in entries:
            kind, rest = ("w", ()) if k < 0 else ("row", (k,))
            parent = (kind, less((dy, dz), e)) + rest
            need = [parent] if parent[1] != (0, 0) else []
            links[e].append(((kind, (dy, dz)) + rest, cost[0] if k < 0 else cost[k], need))
    for dx in (1, 3):
        order = []
        for k in range(parts + 1):
            order.append((("col", dx, k), cost[k], []))
            if k:
                order.append((("far", dx, k - 1), cost[k - 1] / 2, [("col", dx, k - 1)]))
        links[dx] = order + [(("far", dx, parts), cost[parts] / 2, [("col", dx, parts)])]
    links["sib"] = []
    for k in range(parts + 1):
        for dx in (0, 1, 3, 2):
            need = {0: [], 1: [("col", 1, k)], 3: [("col", 3, k)], 2: [("far", 1, k), ("far", 3, k)]}[dx]
            links["sib"].append((("sib", dx, k), cost[k] / 6, need))
    early = [n for v in links.values() for n, _, _ in v if n[0] == "w" or n[0] in ("col", "far", "sib") and n[-1] == 0]
    links["y"] = [(("y",), 6.0, early)]
    return links


def schedule(links):
    arrive, at, free, steps = {}, dict.fromkeys(links, 0), dict.fromkeys(links, 0.0), []
    while any(at[link] < len(links[link]) for link in links):
        for link, order in links.items():
            while at[link] < len(order) and all(n in arrive for n in order[at[link]][2]):
                name, cost, need = order[at[link]]
                ready = max([arrive[n] for n in need], default=0.0)
                paced = arrive[order[at[link] - WINDOW][0]] if at[link] >= WINDOW else 0.0
                free[link] = max(free[link], ready) + cost
                arrive[name] = free[link] + LATENCY
                steps += [(max(ready, paced), 1, name), (arrive[name], 0, name)]
                at[link] += 1
    return sorted(steps, key=lambda v: v[:2])


def kernel(parts, rx_hbm, rs_hbm, cou_hbm, w_hbm, qmap_hbm, qslot_hbm, out,
           rx, cou, qmap, qslot, srow, xrow, scol, xcol, wst, pt, ysend, y, rout, tout, tin, inb, acc,
           lsem, ssem, rsem):
    width = srow.shape[1]
    nb = rx.shape[0]
    chunk = xrow.shape[2]
    kr = lax.axis_index("krow")
    tr = lax.axis_index("tri")
    px, pc = kr // CORES, kr % CORES
    pz, py = tr // SIDE, tr % SIDE

    def plane_at(b):
        return ((pz + b[1]) % SIDE) * SIDE + (py + b[0]) % SIDE

    def line_at(dx, dc):
        return ((px + dx) % SIDE) * CORES + (pc + dc) % CORES

    def block(index):
        return pl.ds(pl.multiple_of(index * nb, nb), nb)

    def row(k, slot):
        rows = pl.ds(slot * nb, nb)
        return srow.at[rows] if k == 0 else xrow.at[k - 1, rows]

    def col(k, o):
        return scol.at[block(o)] if k == 0 else xcol.at[k - 1, block(o)]

    line = [(dx, dc) for dx in range(SIDE) for dc in range(CORES) if (dx, dc) != (0, 0)]
    others = [(dy, dz) for dy in range(SIDE) for dz in range(SIDE) if (dy, dz) != (0, 0)]

    barrier = pltpu.get_barrier_semaphore()
    for b in others:
        pl.semaphore_signal(barrier, inc=1, device_id={"tri": plane_at(b)}, device_id_type=MESH)
    for dx, dc in line:
        pl.semaphore_signal(barrier, inc=1, device_id={"krow": line_at(dx, dc)}, device_id_type=MESH)

    loads = [
        pltpu.make_async_copy(src, dst, lsem.at[i])
        for i, (src, dst) in enumerate((
            (rx_hbm, rx), (cou_hbm, cou), (rs_hbm, srow.at[0:nb]), (rs_hbm, scol.at[block(kr)]),
            (w_hbm.at[block(kr)], wst.at[tr]), (qmap_hbm, qmap), (qslot_hbm, qslot),
        ))
    ]
    for load in loads:
        load.start()

    def scale(k):
        lanes = pl.ds((k - 1) * chunk, chunk)
        own = (rx[:, lanes].astype(jnp.float32) * jnp.sqrt(cou[lanes]).reshape(1, chunk)).astype(jnp.bfloat16)
        xrow[k - 1, 0:nb, :] = own
        xcol[k - 1, block(kr), :] = own

    out[...] = jnp.zeros_like(out)
    for load in loads:
        load.wait()
    pl.semaphore_wait(barrier, len(others) + len(line))

    copies = {}

    def send(name, src, dst, device):
        i = len(copies)
        copies[name] = pltpu.make_async_remote_copy(
            src_ref=src, dst_ref=dst, send_sem=ssem.at[i], recv_sem=rsem.at[i],
            device_id=device, device_id_type=MESH,
        )
        copies[name].start()

    scaled = set()

    def pass_on(name):
        kind = name[0]
        if kind in ("row", "col") and name[-1] not in scaled | {0}:
            scaled.add(name[-1])
            scale(name[-1])
        if kind == "w":
            b, e = name[1], source[name]
            held = wst.at[plane_at(less(b, e))]
            send(name, held, held, {"tri": plane_at((-e[0], -e[1]))})
        elif kind == "row":
            b, k = name[1:]
            e = source[name]
            send(name, row(k, ROWS.index(less(b, e))), row(k, ROWS.index(b)), {"tri": plane_at((-e[0], -e[1]))})
        elif kind == "col":
            dx, k = name[1:]
            send(name, col(k, kr), col(k, kr), {"krow": line_at(-dx, 0)})
        elif kind == "far":
            dx, k = name[1:]
            held = col(k, line_at(dx, 0)).at[pl.ds(0 if dx == 1 else nb // 2, nb // 2)]
            send(name, held, held, {"krow": line_at(-dx, 0)})
        elif kind == "sib":
            dx, k = name[1:]
            held = col(k, line_at(dx, 0))
            send(name, held, held, {"krow": line_at(0, 1)})
        else:
            project()

    def project():
        pt[...] = (
            lax.dot_general(
                wst[...].reshape(PLANE * nb, width), scol[...], (((1,), (1,)), ((), ())),
                preferred_element_type=jnp.float32,
            ) * -0.5
        ).astype(jnp.bfloat16).reshape(pt.shape)
        low = lax.broadcasted_iota(jnp.int32, (nb, 2 * nb), 1) < nb
        for dx, dc in line + [(0, 0)]:
            o = line_at(dx, dc)
            for q in range(GROUPS // 2):
                lanes = pl.ds(q * 2 * nb, 2 * nb)
                first = pt[qslot[qmap[o, 2 * q]], :, lanes]
                second = pt[qslot[qmap[o, 2 * q + 1]], :, lanes]
                ysend[o, :, lanes] = jnp.where(low, first, second)
            if (dx, dc) == (0, 0):
                y[block(kr), :] = ysend[kr]
            else:
                send(("y", dx, dc), ysend.at[o], y.at[block(kr)], {"krow": o})

    def rows_of(group):
        return slice(group * 2 * nb, (group + 1) * 2 * nb)

    def work(group, k):
        rows = rows_of(group)
        if k == 0:
            part = jnp.dot(srow[rows, :], y[...], preferred_element_type=jnp.float32)
        else:
            part = lax.dot_general(
                xrow[k - 1, rows, :], xcol[k - 1], (((1,), (1,)), ((), ())), preferred_element_type=jnp.float32
            )
        total = part if not done[group] else acc[rows, :] + part
        done[group] += 1
        if done[group] <= parts:
            acc[rows, :] = total
        else:
            finish(group, total)

    def finish(group, total):
        rows = rows_of(group)
        total = total * 2.0
        rout[rows, :] = total.astype(jnp.bfloat16)
        for slot in (2 * group, 2 * group + 1):
            b = ROWS[slot]
            if slot in OUT:
                send(("out", b), rout.at[pl.ds(slot * nb, nb)], inb.at[slot], {"tri": plane_at(b)})
        if 2 * group in FLIP:
            i = FLIP.index(2 * group)
            tout[i] = total.T.astype(jnp.bfloat16)
            for dx, dc in line:
                o = line_at(dx, dc)
                send(("flip", i, dx, dc), tout.at[i, block(o)], tin.at[i, block(kr)], {"krow": o})
            tin[i, block(kr), :] = tout[i, block(kr), :]
        sent.append(group)

    upper = lax.broadcasted_iota(jnp.int32, (nb, 2 * nb), 1) // nb
    span = PLANE * nb

    def place(t, o, half, got, turned):
        lanes = pl.ds(pl.multiple_of(o * span + (t // 2) * 2 * nb, 2 * nb), 2 * nb)
        value = jnp.where(t % 2 == half, got, turned)
        out[:, lanes] = jnp.where(upper == t % 2, value, out[:, lanes].astype(jnp.float32)).astype(out.dtype)

    def gather(group):
        for slot in (2 * group, 2 * group + 1):
            if slot in OUT or slot == 0:
                b = ROWS[slot]
                if slot:
                    copies["out", b].wait_recv()
                held = inb.at[slot] if slot else rout.at[0:nb]
                for q in range(GROUPS // 2):
                    got = held[:, q * 2 * nb : (q + 1) * 2 * nb].astype(jnp.float32)
                    turned = pltpu.roll(got, nb, 1)
                    for half in range(2):
                        place(plane_at((-b[0], -b[1])), 2 * q + half, half, got, turned)
        if 2 * group in FLIP:
            i = FLIP.index(2 * group)
            for dx, dc in line:
                copies["flip", i, dx, dc].wait_recv()
            for o in range(GROUPS):
                got = tin[i, o * nb : (o + 1) * nb, :].astype(jnp.float32)
                turned = pltpu.roll(got, nb, 1)
                for half in range(2):
                    place(plane_at(ROWS[2 * group + half]), o, half, got, turned)

    sent = []
    cost = [2 * 2 * nb * (chunk if k else width) / RATE for k in range(parts + 1)]
    links = transfers(parts, cost)
    steps = schedule(links)
    source = {name: link for link, order in links.items() for name, _, _ in order}

    def names(kind, k=None, blocks=None):
        return [n for n in source if n[0] == kind and k in (None, n[-1]) and (blocks is None or n[1] in blocks)]

    def columns(k):
        return names("col", k) + names("far", k) + names("sib", k)

    done = [0] * (len(ROWS) // 2)
    tasks = []
    for k in range(parts + 1):
        for group in range(len(ROWS) // 2):
            blocks = ROWS[2 * group : 2 * group + 2]
            need = names("row", k, blocks) + (columns(k) if k else names("y"))
            tasks.append((set(need), functools.partial(work, group, k)))

    seen = set()
    for _, start, name in steps:
        if start:
            pass_on(name)
            continue
        for copy in [copies["y", dx, dc] for dx, dc in line] if name == ("y",) else [copies[name]]:
            copy.wait_recv()
        seen.add(name)
        for task in [t for t in tasks if seen >= t[0]]:
            task[1]()
            tasks.remove(task)

    while sent:
        gather(sent.pop(0))
    for copy in copies.values():
        copy.wait_send()


def body(rho_x, rho_s, coulomb, screening, qmap, qslot):
    kpoints, npair, waves = rho_x.shape
    width = rho_s.shape[-1]
    nb = kpoints * npair
    parts = PARTS
    chunk = waves // parts
    cols = GROUPS * nb
    bf16, f32 = jnp.bfloat16, jnp.float32
    vmem = pl.BlockSpec(memory_space=pltpu.VMEM)
    hbm = pl.BlockSpec(memory_space=pltpu.HBM)
    ncopies = 15 + (9 + 4 + 4) * (parts + 1) + 7 + len(OUT) + 7 * len(FLIP)
    out = pl.pallas_call(
        functools.partial(kernel, parts),
        out_shape=jax.ShapeDtypeStruct((nb, GROUPS * PLANE * nb), bf16),
        in_specs=[hbm] * 6,
        out_specs=vmem,
        scratch_shapes=[
            pltpu.VMEM((nb, waves), bf16),
            pltpu.VMEM((waves,), f32),
            pltpu.SMEM(qmap.shape, jnp.int32),
            pltpu.SMEM(qslot.shape, jnp.int32),
            pltpu.VMEM((len(ROWS) * nb, width), bf16),
            pltpu.VMEM((parts, len(ROWS) * nb, chunk), bf16),
            pltpu.VMEM((cols, width), bf16),
            pltpu.VMEM((parts, cols, chunk), bf16),
            pltpu.VMEM((PLANE, nb, width), bf16),
            pltpu.VMEM((PLANE, nb, cols), bf16),
            pltpu.VMEM((GROUPS, nb, cols), bf16),
            pltpu.VMEM((width, cols), bf16),
            pltpu.VMEM((len(ROWS) * nb, cols), bf16),
            pltpu.VMEM((len(FLIP), cols, 2 * nb), bf16),
            pltpu.VMEM((len(FLIP), cols, 2 * nb), bf16),
            pltpu.VMEM((len(ROWS), nb, cols), bf16),
            pltpu.VMEM((len(ROWS) * nb, cols), f32),
            pltpu.SemaphoreType.DMA((7,)),
            pltpu.SemaphoreType.DMA((ncopies,)),
            pltpu.SemaphoreType.DMA((ncopies,)),
        ],
        compiler_params=pltpu.CompilerParams(
            collective_id=0, has_side_effects=True, vmem_limit_bytes=62 * 2**20
        ),
        name="kernel_rows",
    )(
        rho_x.reshape(nb, waves),
        rho_s.reshape(nb, width),
        coulomb,
        screening.reshape(width, width),
        qmap,
        qslot,
    )
    return out.astype(f32).reshape(kpoints, npair, -1)


def solution(mesh):
    placed = (
        P(("krow", "tri"), None, None),
        P(("krow", "tri"), None, None),
        P(),
        P("tri", None, None),
        P(),
        P(),
    )
    return jax.shard_map(
        body, mesh=mesh, in_specs=placed, out_specs=P(("krow", "tri"), None, None), check_vma=False
    )
```

time: 70.8 us -> 55.7 us (0.79)
  Pallas kernels: 64.1 us -> 52.8 us
  local copies, waits for them, and re-layouts: 6.23 us -> 0 us
  other arithmetic: 0 us -> 2.68 us
    pallas_call x1, Pallas kernels: 64.1 us -> 52.8 us  [body(): pl.pallas_call(functools.partial(kernel, parts), out_shape=jax.ShapeDtype...]
    unnamed x11 -> x0, local copies, waits for them, and re-layouts: 5.52 us -> none
    reshape x0 -> x1, other arithmetic: none -> 2.68 us  [body(): return out.astype(f32).reshape(kpoints, npair, -1)]
    reshape x1 -> x0, local copies, waits for them, and re-layouts: 0.71 us -> none  [body(): coulomb.reshape(1, waves)]
where the time goes in v2:
time: 55.7 us; the launch traced here: 55.5 us
  Pallas kernels  52.8 us (95%)
  other arithmetic  2.68 us (5%)
    pallas_call x1, Pallas kernels, body(): pl.pallas_call(functools.partial(kernel, parts), out_shape=jax.ShapeDtype...  52.8 us
    reshape x1, other arithmetic, body(): return out.astype(f32).reshape(kpoints, npair, -1)  2.68 us

profile of v2, /device:TPU:1, one launch (start us, length us, event | category | flops | bytes accessed | tf_op | source)
XLA Modules:
  0.0 55.5 jit_solution(10051219257273880190)
XLA Ops:
  0.0 52.8 %kernel_rows.1 = bf16[64,8192]{1,0:T(8,128)(2,1)} custom-call(bf16[64,2688]{1,0:T(8,128)(2,1)} %bitcast.7, bf16[64,512]{1,0:T(8,128)(2,1)} %bitcast.8, f32[2688]{0:T(1024)} %cou_hbm.1, bf16[512,512]{1,0:T(8,128)(2,1)} %bitcast.6, s32[8,8]{1,0:T(8,128)} %qmap_hbm.1, s32[16]{0:T(128)} %qslot_hbm.1), custom_call_target="tpu_custom_call" | custom-call | tf_op jit(solution)/shard_map/kernel_rows/pallas_call | solution.py:318
  52.8 2.7 %convert.1 = f32[4,16,8192]{2,1,0:T(8,128)} convert(bf16[4,16,8192]{2,1,0:T(8,128)(2,1)} %bitcast.5) | non-fusion elementwise | flops 524288 | bytes 3145728 | tf_op jit(solution)/shard_map/reshape | solution.py:357

commit v3 on v2

--- a/solution.py
+++ b/solution.py
@@ -13,31 +13,31 @@
 GROUPS = SIDE * CORES
 PLANE = SIDE * SIDE
 
-ROWS = ((0, 0), (2, 0), (3, 0), (0, 3), (1, 3), (0, 2), (2, 1), (1, 2), (2, 2), (1, 1))
+ROWS = ((0, 0), (0, 2), (0, 1), (1, 0), (2, 0), (2, 2), (2, 3), (3, 1), (3, 2), (3, 3))
 PLAN = {
     (0, 1): (
-        (0, 1, -1), (0, 2, -1), (1, 1, -1), (2, 1, -1), (3, 2, -1), (1, 2, -1), (2, 2, -1), (3, 3, -1),
-        (2, 1, 0), (2, 1, 1), (2, 2, 0), (2, 1, 3), (2, 1, 2), (2, 2, 3),
+        (0, 1, 3), (0, 1, 1), (0, 2, 3), (1, 1, -1), (0, 1, 0), (0, 1, 2), (0, 2, 0), (0, 2, 1),
+        (3, 3, 3), (3, 2, 2), (0, 2, 2), (3, 3, 1),
     ),
     (1, 0): (
-        (1, 0, -1), (2, 0, -1), (1, 3, -1), (1, 3, 2), (1, 3, 1), (2, 3, -1), (1, 2, 2), (1, 2, 1),
-        (1, 3, 3), (1, 3, 0), (2, 2, 1), (2, 2, 2),
+        (1, 0, -1), (1, 0, 1), (1, 0, 2), (1, 2, -1), (1, 0, 0), (2, 0, 2), (2, 0, 0), (2, 0, 1),
+        (1, 0, 3), (3, 3, 2), (2, 0, 3), (3, 3, 0),
     ),
     (0, 3): (
-        (0, 3, -1), (0, 3, 2), (0, 3, 1), (0, 2, 2), (0, 2, 1), (3, 0, -1), (0, 3, 3), (0, 3, 0),
-        (1, 1, 2), (0, 2, 3), (0, 2, 0), (1, 2, 3),
+        (0, 3, -1), (0, 2, -1), (1, 3, -1), (3, 3, -1), (2, 3, -1), (0, 1, -1), (3, 1, -1), (2, 2, -1),
+        (2, 3, 2), (2, 3, 0), (2, 3, 1), (2, 2, 0), (3, 1, 0), (2, 2, 1), (2, 2, 2),
     ),
     (3, 0): (
-        (3, 0, 1), (3, 0, 0), (3, 1, -1), (2, 0, 1), (2, 0, 0), (3, 0, 3), (3, 0, 2), (2, 0, 3),
-        (2, 0, 2), (1, 1, 0), (1, 1, 1), (1, 2, 0), (1, 1, 3),
+        (3, 0, -1), (2, 0, -1), (3, 1, 3), (3, 2, -1), (3, 1, 1), (3, 2, 3), (2, 1, -1), (3, 1, 2),
+        (3, 2, 0), (3, 2, 1), (2, 2, 3), (2, 3, 3),
     ),
 }
-OUT = tuple(i for i, b in enumerate(ROWS) if i == 1 or b[0] % 2 or b[1] % 2)
-FLIP = (2, 4, 6, 8)
+OUT = tuple(i for i, b in enumerate(ROWS) if b[0] % 2 or b[1] % 2)
+FLIP = (0, 2, 4, 6, 8)
 PARTS = 3
-RATE = 9e4
+RATE = 8e4
 LATENCY = 1.9
-WINDOW = 4
+WINDOW = 3
 
 
 def less(b, e):
@@ -132,14 +132,16 @@
         load.start()
 
     def scale(k):
+        if not scaled:
+            loads[0].wait()
+            loads[1].wait()
+        scaled.add(k)
         lanes = pl.ds((k - 1) * chunk, chunk)
         own = (rx[:, lanes].astype(jnp.float32) * jnp.sqrt(cou[lanes]).reshape(1, chunk)).astype(jnp.bfloat16)
         xrow[k - 1, 0:nb, :] = own
         xcol[k - 1, block(kr), :] = own
 
     out[...] = jnp.zeros_like(out)
-    for load in loads:
-        load.wait()
     pl.semaphore_wait(barrier, len(others) + len(line))
 
     copies = {}
@@ -157,19 +159,20 @@
     def pass_on(name):
         kind = name[0]
         if kind in ("row", "col") and name[-1] not in scaled | {0}:
-            scaled.add(name[-1])
             scale(name[-1])
         if kind == "w":
             b, e = name[1], source[name]
             held = wst.at[plane_at(less(b, e))]
-            send(name, held, held, {"tri": plane_at((-e[0], -e[1]))})
+            own = w_hbm.at[block(kr)] if less(b, e) == (0, 0) else held
+            send(name, own, held, {"tri": plane_at((-e[0], -e[1]))})
         elif kind == "row":
             b, k = name[1:]
             e = source[name]
-            send(name, row(k, ROWS.index(less(b, e))), row(k, ROWS.index(b)), {"tri": plane_at((-e[0], -e[1]))})
+            own = rs_hbm if k == 0 and less(b, e) == (0, 0) else row(k, ROWS.index(less(b, e)))
+            send(name, own, row(k, ROWS.index(b)), {"tri": plane_at((-e[0], -e[1]))})
         elif kind == "col":
             dx, k = name[1:]
-            send(name, col(k, kr), col(k, kr), {"krow": line_at(-dx, 0)})
+            send(name, col(k, kr) if k else rs_hbm, col(k, kr), {"krow": line_at(-dx, 0)})
         elif kind == "far":
             dx, k = name[1:]
             held = col(k, line_at(dx, 0)).at[pl.ds(0 if dx == 1 else nb // 2, nb // 2)]
@@ -177,11 +180,13 @@
         elif kind == "sib":
             dx, k = name[1:]
             held = col(k, line_at(dx, 0))
-            send(name, held, held, {"krow": line_at(0, 1)})
+            send(name, rs_hbm if (dx, k) == (0, 0) else held, held, {"krow": line_at(0, 1)})
         else:
             project()
 
     def project():
+        for load in loads[2:]:
+            load.wait()
         pt[...] = (
             lax.dot_general(
                 wst[...].reshape(PLANE * nb, width), scol[...], (((1,), (1,)), ((), ())),
@@ -264,7 +269,8 @@
                 got = tin[i, o * nb : (o + 1) * nb, :].astype(jnp.float32)
                 turned = pltpu.roll(got, nb, 1)
                 for half in range(2):
-                    place(plane_at(ROWS[2 * group + half]), o, half, got, turned)
+                    if 2 * group + half:
+                        place(plane_at(ROWS[2 * group + half]), o, half, got, turned)
 
     sent = []
     cost = [2 * 2 * nb * (chunk if k else width) / RATE for k in range(parts + 1)]
@@ -302,6 +308,20 @@
         gather(sent.pop(0))
     for copy in copies.values():
         copy.wait_send()
+
+
+def widen(pieces, src, dst, held, wide, sem_in, sem_out):
+    rows = src.shape[0] // pieces
+    reads = [pltpu.make_async_copy(src.at[pl.ds(i * rows, rows)], held.at[pl.ds(i * rows, rows)], sem_in.at[i]) for i in range(pieces)]
+    writes = [pltpu.make_async_copy(wide.at[pl.ds(i * rows, rows)], dst.at[pl.ds(i * rows, rows)], sem_out.at[i]) for i in range(pieces)]
+    for read in reads:
+        read.start()
+    for i in range(pieces):
+        reads[i].wait()
+        wide[i * rows : (i + 1) * rows, :] = held[i * rows : (i + 1) * rows, :].astype(wide.dtype)
+        writes[i].start()
+    for write in writes:
+        write.wait()
 
 
 def body(rho_x, rho_s, coulomb, screening, qmap, qslot):
@@ -354,7 +374,22 @@
         qmap,
         qslot,
     )
-    return out.astype(f32).reshape(kpoints, npair, -1)
+    pieces = 4
+    out = pl.pallas_call(
+        functools.partial(widen, pieces),
+        out_shape=jax.ShapeDtypeStruct(out.shape, f32),
+        in_specs=[hbm],
+        out_specs=hbm,
+        scratch_shapes=[
+            pltpu.VMEM(out.shape, bf16),
+            pltpu.VMEM(out.shape, f32),
+            pltpu.SemaphoreType.DMA((pieces,)),
+            pltpu.SemaphoreType.DMA((pieces,)),
+        ],
+        compiler_params=pltpu.CompilerParams(vmem_limit_bytes=62 * 2**20),
+        name="widen",
+    )(out)
+    return out.reshape(kpoints, npair, -1)
 
 
 def solution(mesh):

time: 55.7 us -> 53 us (0.952)
  other arithmetic: 2.68 us -> 0 us
    reshape x1 -> x0, other arithmetic: 2.68 us -> none  [body(): return out.astype(f32).reshape(kpoints, npair, -1)]
    pallas_call x0 -> x1, Pallas kernels: none -> 2.36 us  [body(): pl.pallas_call(functools.partial(widen, pieces), out_shape=jax.ShapeDtype...]
    pallas_call x1, Pallas kernels: 52.8 us -> 50.5 us  [body(): pl.pallas_call(functools.partial(kernel, parts), out_shape=jax.ShapeDtype...]
where the time goes in v3:
time: 53 us; the launch traced here: 52.9 us
  Pallas kernels  52.9 us (100%)
    pallas_call x1, Pallas kernels, body(): pl.pallas_call(functools.partial(kernel, parts), out_shape=jax.ShapeDtype...  50.5 us
    pallas_call x1, Pallas kernels, body(): pl.pallas_call(functools.partial(widen, pieces), out_shape=jax.ShapeDtype...  2.36 us

profile of v3, /device:TPU:1, one launch (start us, length us, event | category | flops | bytes accessed | tf_op | source)
XLA Modules:
  0.0 52.9 jit_solution(12032371190555459754)
XLA Ops:
  0.0 50.5 %kernel_rows.1.src = bf16[64,8192]{1,0:T(8,128)(2,1)} custom-call(bf16[64,2688]{1,0:T(8,128)(2,1)} %bitcast.5, bf16[64,512]{1,0:T(8,128)(2,1)} %bitcast.6, f32[2688]{0:T(1024)} %cou_hbm.1, bf16[512,512]{1,0:T(8,128)(2,1)} %bitcast.4, s32[8,8]{1,0:T(8,128)} %qmap_hbm.1, s32[16]{0:T(128)} %qslot_hbm.1), custom_call_target="tpu_custom_call" | custom-call | tf_op jit(solution)/shard_map/kernel_rows/pallas_call | solution.py:338
  50.5 2.4 %widen.1 = f32[64,8192]{1,0:T(8,128)} custom-call(bf16[64,8192]{1,0:T(8,128)(2,1)} %kernel_rows.1.src), custom_call_target="tpu_custom_call" | custom-call | tf_op jit(solution)/shard_map/widen/pallas_call | solution.py:378

commit v4 on v3

--- a/solution.py
+++ b/solution.py
@@ -77,7 +77,8 @@
             while at[link] < len(order) and all(n in arrive for n in order[at[link]][2]):
                 name, cost, need = order[at[link]]
                 ready = max([arrive[n] for n in need], default=0.0)
-                paced = arrive[order[at[link] - WINDOW][0]] if at[link] >= WINDOW else 0.0
+                depth = WINDOW + (name[-1] == 0 or name[0] == "w")
+                paced = arrive[order[at[link] - depth][0]] if at[link] >= depth else 0.0
                 free[link] = max(free[link], ready) + cost
                 arrive[name] = free[link] + LATENCY
                 steps += [(max(ready, paced), 1, name), (arrive[name], 0, name)]
@@ -85,8 +86,8 @@
     return sorted(steps, key=lambda v: v[:2])
 
 
-def kernel(parts, rx_hbm, rs_hbm, cou_hbm, w_hbm, qmap_hbm, qslot_hbm, out,
-           rx, cou, qmap, qslot, srow, xrow, scol, xcol, wst, pt, ysend, y, rout, tout, tin, inb, acc,
+def kernel(parts, rx_hbm, rs_hbm, cou_hbm, w_hbm, qmap_hbm, qslot_hbm, inb,
+           rx, cou, qmap, qslot, srow, xrow, scol, xcol, wst, pt, ysend, y, rout, tout, tin, acc,
            lsem, ssem, rsem):
     width = srow.shape[1]
     nb = rx.shape[0]
@@ -141,7 +142,6 @@
         xrow[k - 1, 0:nb, :] = own
         xcol[k - 1, block(kr), :] = own
 
-    out[...] = jnp.zeros_like(out)
     pl.semaphore_wait(barrier, len(others) + len(line))
 
     copies = {}
@@ -227,11 +227,6 @@
     def finish(group, total):
         rows = rows_of(group)
         total = total * 2.0
-        rout[rows, :] = total.astype(jnp.bfloat16)
-        for slot in (2 * group, 2 * group + 1):
-            b = ROWS[slot]
-            if slot in OUT:
-                send(("out", b), rout.at[pl.ds(slot * nb, nb)], inb.at[slot], {"tri": plane_at(b)})
         if 2 * group in FLIP:
             i = FLIP.index(2 * group)
             tout[i] = total.T.astype(jnp.bfloat16)
@@ -239,38 +234,25 @@
                 o = line_at(dx, dc)
                 send(("flip", i, dx, dc), tout.at[i, block(o)], tin.at[i, block(kr)], {"krow": o})
             tin[i, block(kr), :] = tout[i, block(kr), :]
+        rout[rows, :] = total.astype(jnp.bfloat16)
+        for slot in (2 * group, 2 * group + 1):
+            b = ROWS[slot]
+            if slot in OUT:
+                send(("out", b), rout.at[pl.ds(slot * nb, nb)], inb.at[tr], {"tri": plane_at(b)})
         sent.append(group)
 
-    upper = lax.broadcasted_iota(jnp.int32, (nb, 2 * nb), 1) // nb
-    span = PLANE * nb
-
-    def place(t, o, half, got, turned):
-        lanes = pl.ds(pl.multiple_of(o * span + (t // 2) * 2 * nb, 2 * nb), 2 * nb)
-        value = jnp.where(t % 2 == half, got, turned)
-        out[:, lanes] = jnp.where(upper == t % 2, value, out[:, lanes].astype(jnp.float32)).astype(out.dtype)
-
     def gather(group):
-        for slot in (2 * group, 2 * group + 1):
-            if slot in OUT or slot == 0:
-                b = ROWS[slot]
-                if slot:
-                    copies["out", b].wait_recv()
-                held = inb.at[slot] if slot else rout.at[0:nb]
-                for q in range(GROUPS // 2):
-                    got = held[:, q * 2 * nb : (q + 1) * 2 * nb].astype(jnp.float32)
-                    turned = pltpu.roll(got, nb, 1)
-                    for half in range(2):
-                        place(plane_at((-b[0], -b[1])), 2 * q + half, half, got, turned)
+        if group == 0:
+            inb[tr] = rout[0:nb, :]
         if 2 * group in FLIP:
             i = FLIP.index(2 * group)
             for dx, dc in line:
                 copies["flip", i, dx, dc].wait_recv()
-            for o in range(GROUPS):
-                got = tin[i, o * nb : (o + 1) * nb, :].astype(jnp.float32)
-                turned = pltpu.roll(got, nb, 1)
+            for q in range(GROUPS // 2):
+                got = mix(tin[i, 2 * q * nb : (2 * q + 1) * nb, :], tin[i, (2 * q + 1) * nb : (2 * q + 2) * nb, :])
                 for half in range(2):
                     if 2 * group + half:
-                        place(plane_at(ROWS[2 * group + half]), o, half, got, turned)
+                        inb[plane_at(ROWS[2 * group + half]), :, q * 2 * nb : (q + 1) * 2 * nb] = got[half].astype(inb.dtype)
 
     sent = []
     cost = [2 * 2 * nb * (chunk if k else width) / RATE for k in range(parts + 1)]
@@ -306,20 +288,37 @@
 
     while sent:
         gather(sent.pop(0))
+    for slot in OUT:
+        copies["out", ROWS[slot]].wait_recv()
     for copy in copies.values():
         copy.wait_send()
 
 
-def widen(pieces, src, dst, held, wide, sem_in, sem_out):
-    rows = src.shape[0] // pieces
-    reads = [pltpu.make_async_copy(src.at[pl.ds(i * rows, rows)], held.at[pl.ds(i * rows, rows)], sem_in.at[i]) for i in range(pieces)]
-    writes = [pltpu.make_async_copy(wide.at[pl.ds(i * rows, rows)], dst.at[pl.ds(i * rows, rows)], sem_out.at[i]) for i in range(pieces)]
+def mix(first, second):
+    nb = first.shape[0]
+    low = lax.broadcasted_iota(jnp.int32, first.shape, 1) < nb
+    first, second = first.astype(jnp.float32), second.astype(jnp.float32)
+    return jnp.where(low, first, pltpu.roll(second, nb, 1)), jnp.where(low, pltpu.roll(first, nb, 1), second)
+
+
+def widen(src, dst, held, wide, sem_in, sem_out):
+    pieces, plane, nb, tile = held.shape
+    span = plane * nb
+    reads = [
+        pltpu.make_async_copy(src.at[:, :, pl.ds(q * tile, tile)], held.at[q], sem_in.at[q]) for q in range(pieces)
+    ]
+    writes = [
+        pltpu.make_async_copy(wide.at[q], dst.at[:, pl.ds(q * 2 * span, 2 * span)], sem_out.at[q]) for q in range(pieces)
+    ]
     for read in reads:
         read.start()
-    for i in range(pieces):
-        reads[i].wait()
-        wide[i * rows : (i + 1) * rows, :] = held[i * rows : (i + 1) * rows, :].astype(wide.dtype)
-        writes[i].start()
+    for q in range(pieces):
+        reads[q].wait()
+        for m in range(plane // 2):
+            for half, got in enumerate(mix(held[q, 2 * m], held[q, 2 * m + 1])):
+                at = half * span + m * tile
+                wide[q, :, at : at + tile] = got
+        writes[q].start()
     for write in writes:
         write.wait()
 
@@ -337,7 +336,7 @@
     ncopies = 15 + (9 + 4 + 4) * (parts + 1) + 7 + len(OUT) + 7 * len(FLIP)
     out = pl.pallas_call(
         functools.partial(kernel, parts),
-        out_shape=jax.ShapeDtypeStruct((nb, GROUPS * PLANE * nb), bf16),
+        out_shape=jax.ShapeDtypeStruct((PLANE, nb, cols), bf16),
         in_specs=[hbm] * 6,
         out_specs=vmem,
         scratch_shapes=[
@@ -356,7 +355,6 @@
             pltpu.VMEM((len(ROWS) * nb, cols), bf16),
             pltpu.VMEM((len(FLIP), cols, 2 * nb), bf16),
             pltpu.VMEM((len(FLIP), cols, 2 * nb), bf16),
-            pltpu.VMEM((len(ROWS), nb, cols), bf16),
             pltpu.VMEM((len(ROWS) * nb, cols), f32),
             pltpu.SemaphoreType.DMA((7,)),
             pltpu.SemaphoreType.DMA((ncopies,)),
@@ -374,15 +372,15 @@
         qmap,
         qslot,
     )
-    pieces = 4
+    pieces = GROUPS // 2
     out = pl.pallas_call(
-        functools.partial(widen, pieces),
-        out_shape=jax.ShapeDtypeStruct(out.shape, f32),
+        widen,
+        out_shape=jax.ShapeDtypeStruct((nb, PLANE * cols), f32),
         in_specs=[hbm],
         out_specs=hbm,
         scratch_shapes=[
-            pltpu.VMEM(out.shape, bf16),
-            pltpu.VMEM(out.shape, f32),
+            pltpu.VMEM((pieces, PLANE, nb, 2 * nb), bf16),
+            pltpu.VMEM((pieces, nb, PLANE * cols // pieces), f32),
             pltpu.SemaphoreType.DMA((pieces,)),
             pltpu.SemaphoreType.DMA((pieces,)),
         ],

time: 53 us -> 52.6 us (level)
  no operation moved by 1% of the time
where the time goes in v4:
time: 52.6 us; the launch traced here: 52.5 us
  Pallas kernels  52.5 us (100%)
    pallas_call x1, Pallas kernels, body(): pl.pallas_call(functools.partial(kernel, parts), out_shape=jax.ShapeDtype...  50 us
    pallas_call x1, Pallas kernels, body(): pl.pallas_call(widen, out_shape=jax.ShapeDtypeStruct((nb, PLANE * cols),...  2.48 us

profile of v4, /device:TPU:1, one launch (start us, length us, event | category | flops | bytes accessed | tf_op | source)
XLA Modules:
  0.0 52.5 jit_solution(15155107913094617016)
XLA Ops:
  0.0 50.0 %kernel_rows.1.src = bf16[16,64,512]{2,1,0:T(8,128)(2,1)} custom-call(bf16[64,2688]{1,0:T(8,128)(2,1)} %bitcast.5, bf16[64,512]{1,0:T(8,128)(2,1)} %bitcast.6, f32[2688]{0:T(1024)} %cou_hbm.1, bf16[512,512]{1,0:T(8,128)(2,1)} %bitcast.4, s32[8,8]{1,0:T(8,128)} %qmap_hbm.1, s32[16]{0:T(128)} %qslot_hbm.1), custom_call_target="tpu_custom_call" | custom-call | tf_op jit(solution)/shard_map/kernel_rows/pallas_call | solution.py:337
  50.0 2.5 %widen.1 = f32[64,8192]{1,0:T(8,128)} custom-call(bf16[16,64,512]{2,1,0:T(8,128)(2,1)} %kernel_rows.1.src), custom_call_target="tpu_custom_call" | custom-call | tf_op jit(solution)/shard_map/widen/pallas_call | solution.py:376

commit v5 on v4

--- a/solution.py
+++ b/solution.py
@@ -77,8 +77,9 @@
             while at[link] < len(order) and all(n in arrive for n in order[at[link]][2]):
                 name, cost, need = order[at[link]]
                 ready = max([arrive[n] for n in need], default=0.0)
-                depth = WINDOW + (name[-1] == 0 or name[0] == "w")
-                paced = arrive[order[at[link] - depth][0]] if at[link] >= depth else 0.0
+                before = [n for n, _, _ in order[: at[link]] if n[0] != "w"]
+                depth = WINDOW + (name[-1] == 0)
+                paced = arrive[before[-depth]] if len(before) >= depth and name[0] != "w" else 0.0
                 free[link] = max(free[link], ready) + cost
                 arrive[name] = free[link] + LATENCY
                 steps += [(max(ready, paced), 1, name), (arrive[name], 0, name)]

time: 52.6 us -> 53.4 us (1.015)
  Pallas kernels: 52.5 us -> 53.3 us
    pallas_call x1, Pallas kernels: 50 us -> 50.8 us  [body(): pl.pallas_call(functools.partial(kernel, parts), out_shape=jax.ShapeDtype...]
where the time goes in v5:
time: 53.4 us; the launch traced here: 53.3 us
  Pallas kernels  53.3 us (100%)
    pallas_call x1, Pallas kernels, body(): pl.pallas_call(functools.partial(kernel, parts), out_shape=jax.ShapeDtype...  50.8 us
    pallas_call x1, Pallas kernels, body(): pl.pallas_call(widen, out_shape=jax.ShapeDtypeStruct((nb, PLANE * cols),...  2.48 us

profile of v5, /device:TPU:1, one launch (start us, length us, event | category | flops | bytes accessed | tf_op | source)
XLA Modules:
  0.0 53.3 jit_solution(6682970761382971109)
XLA Ops:
  0.0 50.8 %kernel_rows.1.src = bf16[16,64,512]{2,1,0:T(8,128)(2,1)} custom-call(bf16[64,2688]{1,0:T(8,128)(2,1)} %bitcast.5, bf16[64,512]{1,0:T(8,128)(2,1)} %bitcast.6, f32[2688]{0:T(1024)} %cou_hbm.1, bf16[512,512]{1,0:T(8,128)(2,1)} %bitcast.4, s32[8,8]{1,0:T(8,128)} %qmap_hbm.1, s32[16]{0:T(128)} %qslot_hbm.1), custom_call_target="tpu_custom_call" | custom-call | tf_op jit(solution)/shard_map/kernel_rows/pallas_call | solution.py:338
  50.8 2.5 %widen.1 = f32[64,8192]{1,0:T(8,128)} custom-call(bf16[16,64,512]{2,1,0:T(8,128)(2,1)} %kernel_rows.1.src), custom_call_target="tpu_custom_call" | custom-call | tf_op jit(solution)/shard_map/widen/pallas_call | solution.py:377
